TPU v7x, 512 devices: a whole 4x4x16 slice. The times are simulated.
512 devices in a mesh: batch: 128 (over y, z, core), width: 4 (over x).
Axes of the slice: x: 4, y: 4, z: 16, core: 2. Of those that a mesh axis runs over, the one named last changes fastest.
Arguments:
- teacher: bfloat16 [32768, 4096], P('batch', 'width'), may hold values from -48 to 48, as said below
- student: bfloat16 [32768, 1024], P('batch', 'width'), may hold values from -48 to 48, as said below
Outputs:
- grad: float32 [32768, 1024], P('batch', 'width')
Inputs may be any that keep to these rules, and one draw needn't show every extreme that they name: `teacher`: Real-valued embeddings. `student`: Real-valued embeddings.
All inputs are finite; a program needn't handle non-finite values.
Results may differ from a plain program's by a relative error of at most 0.00075.
Values may be sent and summed in bfloat16 or wider, within the bound.
A program may use at most 64 MiB of HBM per device.

v0:
```python
import jax
import jax.numpy as jnp
import numpy as np
from jax import lax
from jax.sharding import PartitionSpec as P

DT = 4096
DS = 1024
REACH = 4


def passed_along(block, axis, distance):
    devices = range(lax.axis_size(axis))
    route = [(i - distance, i) for i in devices if i - distance in devices]
    return lax.ppermute(block, axis, route)


def body(teacher, student):
    group = lax.axis_size("batch")
    owner = lax.axis_index("batch")
    rows_dev = teacher.shape[0]
    teacher_list = [teacher]
    student_list = [student]
    moving = (teacher, student)
    for offset in range(REACH):
        moving = passed_along((moving[0], moving[1]), "batch", -1)
        teacher_list.append(moving[0])
        student_list.append(moving[1])
    offset_list = list(range(REACH + 1))
    moving = (teacher, student)
    for offset in range(REACH):
        moving = passed_along((moving[0], moving[1]), "batch", 1)
        teacher_list.insert(0, moving[0])
        student_list.insert(0, moving[1])
        offset_list.insert(0, -(offset + 1))
    band_teacher = jnp.stack(teacher_list, axis=0)
    band_student = jnp.stack(student_list, axis=0)
    own_tsq = jnp.sum(jnp.square(teacher.astype(jnp.float32)), axis=1) / DT
    own_ssq = jnp.sum(jnp.square(student.astype(jnp.float32)), axis=1) / DS
    band_tsq = jnp.sum(jnp.square(band_teacher.astype(jnp.float32)), axis=2) / DT
    band_ssq = jnp.sum(jnp.square(band_student.astype(jnp.float32)), axis=2) / DS
    tgram = jnp.einsum("rk,wck->wrc", teacher, band_teacher, preferred_element_type=jnp.float32)
    sgram = jnp.einsum("rk,wck->wrc", student, band_student, preferred_element_type=jnp.float32)
    student_part = own_ssq[None, :, None] + band_ssq[:, None, :] - 2.0 * sgram / DS
    teacher_part = own_tsq[None, :, None] + band_tsq[:, None, :] - 2.0 * tgram / DT
    shard_terms = student_part - teacher_part
    partner = owner + jnp.asarray(np.array(offset_list, dtype=np.int32))
    valid = jnp.logical_and(partner >= 0, partner < group)
    residual = lax.psum(shard_terms, "width")
    residual = jnp.where(valid[:, None, None], residual, jnp.zeros_like(residual))
    residual_low = residual.astype(jnp.bfloat16)
    row_total = jnp.sum(residual, axis=(0, 2))
    pulled = jnp.einsum(
        "wrc,wck->rk", residual_low, band_student, preferred_element_type=jnp.float32
    )
    near_count = (2 * REACH + 1) * rows_dev
    grad = (student.astype(jnp.float32) * row_total[:, None] - pulled) / near_count
    return grad


def solution(mesh):
    in_specs = (P("batch", "width"), P("batch", "width"))
    out_specs = P("batch", "width")
    return jax.shard_map(body, mesh=mesh, in_specs=in_specs, out_specs=out_specs, check_vma=False)
```

profile of v0, /device:TPU:25, one launch (start us, length us, event | category | flops | bytes accessed | tf_op | source)
XLA Modules:
  0.0 181.5 jit_solution(11378347629760379573)
XLA Ops:
  6.5 0.0 copy-start.1
  6.5 0.0 all-reduce.2.cloned.1.call-start
  6.5 4.2 %collective-permute-start = (bf16[256,256]{1,0:T(8,128)(2,1)}, bf16[256,256]{1,0:T(8,128)(2,1)S(1)}, u32[]{:S(2)}, u32[]{:S(2)}) collective-permute-start(bf16[256,256]{1,0:T(8,128)(2,1)} %param.4), channel_id=1, source_target_pairs={{0,4},{4,8},{8,12},{12,16},{16,20},{20,24},{24,28},{28,32},{32,36}... | collective-permute-start | bytes 393224 | tf_op jit(solution)/shard_map/ppermute | solution.py:15
  10.8 1.9 %collective-permute-start.4 = (bf16[256,256]{1,0:T(8,128)(2,1)}, bf16[256,256]{1,0:T(8,128)(2,1)S(1)}, u32[]{:S(2)}, u32[]{:S(2)}) collective-permute-start(bf16[256,256]{1,0:T(8,128)(2,1)} %param.4), channel_id=1, source_target_pairs={{4,0},{8,4},{12,8},{16,12},{20,16},{24,20},{28,24},{32,28},{36,32}... | collective-permute-start | bytes 393224 | tf_op jit(solution)/shard_map/ppermute | solution.py:15
  12.7 3.6 %collective-permute-start.8 = (bf16[256,1024]{1,0:T(8,128)(2,1)}, bf16[256,1024]{1,0:T(8,128)(2,1)S(1)}, u32[]{:S(2)}, u32[]{:S(2)}) collective-permute-start(bf16[256,1024]{1,0:T(8,128)(2,1)} %param.3), channel_id=1, source_target_pairs={{0,4},{4,8},{8,12},{12,16},{16,20},{20,24},{24,28},{28,32},{32,36}... | collective-permute-start | bytes 1572872 | tf_op jit(solution)/shard_map/ppermute | solution.py:15
  16.4 7.8 %collective-permute-start.12 = (bf16[256,1024]{1,0:T(8,128)(2,1)}, bf16[256,1024]{1,0:T(8,128)(2,1)S(1)}, u32[]{:S(2)}, u32[]{:S(2)}) collective-permute-start(bf16[256,1024]{1,0:T(8,128)(2,1)} %param.3), channel_id=1, source_target_pairs={{4,0},{8,4},{12,8},{16,12},{20,16},{24,20},{28,24},{32,28},{36,32}... | collective-permute-start | bytes 1572872 | tf_op jit(solution)/shard_map/ppermute | solution.py:15
  24.1 0.0 collective-permute-done
  24.2 1.9 %collective-permute-start.1 = (bf16[256,256]{1,0:T(8,128)(2,1)S(1)}, bf16[256,256]{1,0:T(8,128)(2,1)S(1)}, u32[]{:S(2)}, u32[]{:S(2)}) collective-permute-start(bf16[256,256]{1,0:T(8,128)(2,1)S(1)} %collective-permute-done), channel_id=1, source_target_pairs={{0,4},{4,8},{8,12},{12,16},{16,20},{20,24},{24,28},{28,32},{32,36}... | collective-permute-start | bytes 393224 | tf_op jit(solution)/shard_map/ppermute | solution.py:15
  26.1 1.2 multiply_reduce_fusion.2
  27.3 0.0 collective-permute-done.4
  27.3 5.8 %collective-permute-start.5 = (bf16[256,256]{1,0:T(8,128)(2,1)S(1)}, bf16[256,256]{1,0:T(8,128)(2,1)S(1)}, u32[]{:S(2)}, u32[]{:S(2)}) collective-permute-start(bf16[256,256]{1,0:T(8,128)(2,1)S(1)} %collective-permute-done.4), channel_id=1, source_target_pairs={{4,0},{8,4},{12,8},{16,12},{20,16},{24,20},{28,24},{32,28},{36,32}... | collective-permute-start | bytes 393224 | tf_op jit(solution)/shard_map/ppermute | solution.py:15
  33.1 0.0 collective-permute-done.1
  33.1 1.9 %collective-permute-start.2 = (bf16[256,256]{1,0:T(8,128)(2,1)S(1)}, bf16[256,256]{1,0:T(8,128)(2,1)S(1)}, u32[]{:S(2)}, u32[]{:S(2)}) collective-permute-start(bf16[256,256]{1,0:T(8,128)(2,1)S(1)} %collective-permute-done.1), channel_id=1, source_target_pairs={{0,4},{4,8},{8,12},{12,16},{16,20},{20,24},{24,28},{28,32},{32,36}... | collective-permute-start | bytes 393224 | tf_op jit(solution)/shard_map/ppermute | solution.py:15
  35.0 1.0 fusion.8
  36.0 0.0 collective-permute-done.5
  36.1 5.8 %collective-permute-start.6 = (bf16[256,256]{1,0:T(8,128)(2,1)S(1)}, bf16[256,256]{1,0:T(8,128)(2,1)S(1)}, u32[]{:S(2)}, u32[]{:S(2)}) collective-permute-start(bf16[256,256]{1,0:T(8,128)(2,1)S(1)} %collective-permute-done.5), channel_id=1, source_target_pairs={{4,0},{8,4},{12,8},{16,12},{20,16},{24,20},{28,24},{32,28},{36,32}... | collective-permute-start | bytes 393224 | tf_op jit(solution)/shard_map/ppermute | solution.py:15
  41.8 0.0 collective-permute-done.2
  41.8 1.9 %collective-permute-start.3 = (bf16[256,256]{1,0:T(8,128)(2,1)S(1)}, bf16[256,256]{1,0:T(8,128)(2,1)S(1)}, u32[]{:S(2)}, u32[]{:S(2)}) collective-permute-start(bf16[256,256]{1,0:T(8,128)(2,1)S(1)} %collective-permute-done.2), channel_id=1, source_target_pairs={{0,4},{4,8},{8,12},{12,16},{16,20},{20,24},{24,28},{28,32},{32,36}... | collective-permute-start | bytes 393224 | tf_op jit(solution)/shard_map/ppermute | solution.py:15
  43.8 0.0 collective-permute-done.6
  43.8 6.3 %collective-permute-start.7 = (bf16[256,256]{1,0:T(8,128)(2,1)S(1)}, bf16[256,256]{1,0:T(8,128)(2,1)S(1)}, u32[]{:S(2)}, u32[]{:S(2)}) collective-permute-start(bf16[256,256]{1,0:T(8,128)(2,1)S(1)} %collective-permute-done.6), channel_id=1, source_target_pairs={{4,0},{8,4},{12,8},{16,12},{20,16},{24,20},{28,24},{32,28},{36,32}... | collective-permute-start | bytes 393224 | tf_op jit(solution)/shard_map/ppermute | solution.py:15
  50.1 0.0 collective-permute-done.3
  50.1 0.0 collective-permute-done.8
  50.1 1.9 %collective-permute-start.9 = (bf16[256,1024]{1,0:T(8,128)(2,1)S(1)}, bf16[256,1024]{1,0:T(8,128)(2,1)S(1)}, u32[]{:S(2)}, u32[]{:S(2)}) collective-permute-start(bf16[256,1024]{1,0:T(8,128)(2,1)S(1)} %collective-permute-done.8), channel_id=1, source_target_pairs={{0,4},{4,8},{8,12},{12,16},{16,20},{20,24},{24,28},{28,32},{32,36}... | collective-permute-start | bytes 1572872 | tf_op jit(solution)/shard_map/ppermute | solution.py:15
  52.1 0.9 bitcast_dynamic-update-slice_fusion.13
  53.0 0.0 collective-permute-done.12
  53.0 5.9 %collective-permute-start.13 = (bf16[256,1024]{1,0:T(8,128)(2,1)S(1)}, bf16[256,1024]{1,0:T(8,128)(2,1)S(1)}, u32[]{:S(2)}, u32[]{:S(2)}) collective-permute-start(bf16[256,1024]{1,0:T(8,128)(2,1)S(1)} %collective-permute-done.12), channel_id=1, source_target_pairs={{4,0},{8,4},{12,8},{16,12},{20,16},{24,20},{28,24},{32,28},{36,32}... | collective-permute-start | bytes 1572872 | tf_op jit(solution)/shard_map/ppermute | solution.py:15
  59.0 0.0 collective-permute-done.9
  59.0 3.6 %collective-permute-start.10 = (bf16[256,1024]{1,0:T(8,128)(2,1)S(1)}, bf16[256,1024]{1,0:T(8,128)(2,1)S(1)}, u32[]{:S(2)}, u32[]{:S(2)}) collective-permute-start(bf16[256,1024]{1,0:T(8,128)(2,1)S(1)} %collective-permute-done.9), channel_id=1, source_target_pairs={{0,4},{4,8},{8,12},{12,16},{16,20},{20,24},{24,28},{28,32},{32,36}... | collective-permute-start | bytes 1572872 | tf_op jit(solution)/shard_map/ppermute | solution.py:15
  62.6 0.0 collective-permute-done.7
  62.6 0.4 multiply_reduce_fusion.1
  63.0 0.8 collective-permute-done.13
  63.8 7.5 %collective-permute-start.14 = (bf16[256,1024]{1,0:T(8,128)(2,1)S(1)}, bf16[256,1024]{1,0:T(8,128)(2,1)S(1)}, u32[]{:S(2)}, u32[]{:S(2)}) collective-permute-start(bf16[256,1024]{1,0:T(8,128)(2,1)S(1)} %collective-permute-done.13), channel_id=1, source_target_pairs={{4,0},{8,4},{12,8},{16,12},{20,16},{24,20},{28,24},{32,28},{36,32}... | collective-permute-start | bytes 1572872 | tf_op jit(solution)/shard_map/ppermute | solution.py:15
  71.3 0.0 collective-permute-done.10
  71.4 1.9 %collective-permute-start.11 = (bf16[256,1024]{1,0:T(8,128)(2,1)S(1)}, bf16[256,1024]{1,0:T(8,128)(2,1)S(1)}, u32[]{:S(2)}, u32[]{:S(2)}) collective-permute-start(bf16[256,1024]{1,0:T(8,128)(2,1)S(1)} %collective-permute-done.10), channel_id=1, source_target_pairs={{0,4},{4,8},{8,12},{12,16},{16,20},{20,24},{24,28},{28,32},{32,36}... | collective-permute-start | bytes 1572872 | tf_op jit(solution)/shard_map/ppermute | solution.py:15
  73.3 0.0 copy-done.1
  73.3 0.5 fusion.9
  73.8 0.0 copy-start.2
  73.8 0.8 collective-permute-done.14
  74.6 9.3 %collective-permute-start.15 = (bf16[256,1024]{1,0:T(8,128)(2,1)S(1)}, bf16[256,1024]{1,0:T(8,128)(2,1)S(1)}, u32[]{:S(2)}, u32[]{:S(2)}) collective-permute-start(bf16[256,1024]{1,0:T(8,128)(2,1)S(1)} %collective-permute-done.14), channel_id=1, source_target_pairs={{4,0},{8,4},{12,8},{16,12},{20,16},{24,20},{28,24},{32,28},{36,32}... | collective-permute-start | bytes 1572872 | tf_op jit(solution)/shard_map/ppermute | solution.py:15
  83.9 0.0 collective-permute-done.11
  84.1 0.0 copy-done.2
  84.3 1.1 collective-permute-done.15
  85.5 1.0 multiply_reduce_fusion
  86.5 3.0 %fusion = f32[9,256,256]{1,2,0:T(8,128)} fusion(f32[9,256,256]{2,1,0:T(8,128)S(1)} %fusion.9, bf16[9,256,1024]{2,1,0:T(8,128)(2,1)S(1)} %bitcast_dynamic-update-slice_fusion, f32[9,256]{1,0:T(8,128)S(1)} %broadcast_multiply_fusion, f32[256]{0:T(256)S(1)} %broadcast_multiply_fusion.2, f32[9,256]{1,0:T(8,128)S(1)} %broadcast_multiply_fusion.1, ...), kind=kOutput, calls=%fused_computation.2 | convolution fusion | flops 1212088320 | bytes 9981952 | tf_op jit(solution)/shard_map/rk,wck->wrc/dot_general | solution.py:42
  89.5 0.0 copy-start.3
  89.5 0.0 all-reduce.2.cloned.1.call-update
  89.5 0.6 copy-done.3
  90.2 80.6 %all-reduce.2.cloned.1.call-done = f32[9,256,256]{1,2,0:T(8,128)} async-done(((f32[9,256,256]{1,2,0:T(8,128)}), f32[9,256,256]{1,2,0:T(8,128)}) %all-reduce.2.cloned.1.call-update) | async-done | bytes 2359312 | tf_op jit(solution)/shard_map/psum | solution.py:49
  170.8 0.0 copy-start
  170.8 2.2 %select_reduce_fusion = f32[256]{0:T(256)S(1)} fusion(f32[9,256,256]{1,2,0:T(8,128)} %all-reduce.2.cloned.1.call-done, pred[9]{0:T(512)(128)(4,1)S(1)} %compare_and_fusion), kind=kLoop, calls=%fused_computation.6 | loop fusion | flops 1179392 | bytes 2360329 | tf_op jit(solution)/shard_map/reduce_sum | solution.py:52
  173.1 0.1 copy-done
  173.2 1.4 fusion.6
  (22 shorter events, 0.4 us)
Async XLA Ops:
  6.5 66.8 %copy-start.1 = (bf16[256,256]{1,0:T(8,128)(2,1)S(1)}, bf16[256,256]{1,0:T(8,128)(2,1)}, u32[]{:S(2)}) copy-start(bf16[256,256]{1,0:T(8,128)(2,1)} %param.4) | copy-start | bytes 393220
  6.5 164.3 %all-reduce.2.cloned.1.call-start = ((), (), s32[]{:S(2)}) async-start(), calls=%async_computation | async-start | bytes 4718592 | tf_op jit(solution)/shard_map/psum | solution.py:49
  6.5 17.6 %collective-permute-start = (bf16[256,256]{1,0:T(8,128)(2,1)}, bf16[256,256]{1,0:T(8,128)(2,1)S(1)}, u32[]{:S(2)}, u32[]{:S(2)}) collective-permute-start(bf16[256,256]{1,0:T(8,128)(2,1)} %param.4), channel_id=1, source_target_pairs={{0,4},{4,8},{8,12},{12,16},{16,20},{20,24},{24,28},{28,32},{32,36}... | collective-permute-start | bytes 393224 | tf_op jit(solution)/shard_map/ppermute | solution.py:15
  10.8 16.5 %collective-permute-start.4 = (bf16[256,256]{1,0:T(8,128)(2,1)}, bf16[256,256]{1,0:T(8,128)(2,1)S(1)}, u32[]{:S(2)}, u32[]{:S(2)}) collective-permute-start(bf16[256,256]{1,0:T(8,128)(2,1)} %param.4), channel_id=1, source_target_pairs={{4,0},{8,4},{12,8},{16,12},{20,16},{24,20},{28,24},{32,28},{36,32}... | collective-permute-start | bytes 393224 | tf_op jit(solution)/shard_map/ppermute | solution.py:15
  12.7 37.4 %collective-permute-start.8 = (bf16[256,1024]{1,0:T(8,128)(2,1)}, bf16[256,1024]{1,0:T(8,128)(2,1)S(1)}, u32[]{:S(2)}, u32[]{:S(2)}) collective-permute-start(bf16[256,1024]{1,0:T(8,128)(2,1)} %param.3), channel_id=1, source_target_pairs={{0,4},{4,8},{8,12},{12,16},{16,20},{20,24},{24,28},{28,32},{32,36}... | collective-permute-start | bytes 1572872 | tf_op jit(solution)/shard_map/ppermute | solution.py:15
  16.4 36.7 %collective-permute-start.12 = (bf16[256,1024]{1,0:T(8,128)(2,1)}, bf16[256,1024]{1,0:T(8,128)(2,1)S(1)}, u32[]{:S(2)}, u32[]{:S(2)}) collective-permute-start(bf16[256,1024]{1,0:T(8,128)(2,1)} %param.3), channel_id=1, source_target_pairs={{4,0},{8,4},{12,8},{16,12},{20,16},{24,20},{28,24},{32,28},{36,32}... | collective-permute-start | bytes 1572872 | tf_op jit(solution)/shard_map/ppermute | solution.py:15
  24.2 8.9 %collective-permute-start.1 = (bf16[256,256]{1,0:T(8,128)(2,1)S(1)}, bf16[256,256]{1,0:T(8,128)(2,1)S(1)}, u32[]{:S(2)}, u32[]{:S(2)}) collective-permute-start(bf16[256,256]{1,0:T(8,128)(2,1)S(1)} %collective-permute-done), channel_id=1, source_target_pairs={{0,4},{4,8},{8,12},{12,16},{16,20},{20,24},{24,28},{28,32},{32,36}... | collective-permute-start | bytes 393224 | tf_op jit(solution)/shard_map/ppermute | solution.py:15
  27.3 8.7 %collective-permute-start.5 = (bf16[256,256]{1,0:T(8,128)(2,1)S(1)}, bf16[256,256]{1,0:T(8,128)(2,1)S(1)}, u32[]{:S(2)}, u32[]{:S(2)}) collective-permute-start(bf16[256,256]{1,0:T(8,128)(2,1)S(1)} %collective-permute-done.4), channel_id=1, source_target_pairs={{4,0},{8,4},{12,8},{16,12},{20,16},{24,20},{28,24},{32,28},{36,32}... | collective-permute-start | bytes 393224 | tf_op jit(solution)/shard_map/ppermute | solution.py:15
  33.1 8.7 %collective-permute-start.2 = (bf16[256,256]{1,0:T(8,128)(2,1)S(1)}, bf16[256,256]{1,0:T(8,128)(2,1)S(1)}, u32[]{:S(2)}, u32[]{:S(2)}) collective-permute-start(bf16[256,256]{1,0:T(8,128)(2,1)S(1)} %collective-permute-done.1), channel_id=1, source_target_pairs={{0,4},{4,8},{8,12},{12,16},{16,20},{20,24},{24,28},{28,32},{32,36}... | collective-permute-start | bytes 393224 | tf_op jit(solution)/shard_map/ppermute | solution.py:15
  36.1 7.7 %collective-permute-start.6 = (bf16[256,256]{1,0:T(8,128)(2,1)S(1)}, bf16[256,256]{1,0:T(8,128)(2,1)S(1)}, u32[]{:S(2)}, u32[]{:S(2)}) collective-permute-start(bf16[256,256]{1,0:T(8,128)(2,1)S(1)} %collective-permute-done.5), channel_id=1, source_target_pairs={{4,0},{8,4},{12,8},{16,12},{20,16},{24,20},{28,24},{32,28},{36,32}... | collective-permute-start | bytes 393224 | tf_op jit(solution)/shard_map/ppermute | solution.py:15
  41.8 8.2 %collective-permute-start.3 = (bf16[256,256]{1,0:T(8,128)(2,1)S(1)}, bf16[256,256]{1,0:T(8,128)(2,1)S(1)}, u32[]{:S(2)}, u32[]{:S(2)}) collective-permute-start(bf16[256,256]{1,0:T(8,128)(2,1)S(1)} %collective-permute-done.2), channel_id=1, source_target_pairs={{0,4},{4,8},{8,12},{12,16},{16,20},{20,24},{24,28},{28,32},{32,36}... | collective-permute-start | bytes 393224 | tf_op jit(solution)/shard_map/ppermute | solution.py:15
  43.8 18.8 %collective-permute-start.7 = (bf16[256,256]{1,0:T(8,128)(2,1)S(1)}, bf16[256,256]{1,0:T(8,128)(2,1)S(1)}, u32[]{:S(2)}, u32[]{:S(2)}) collective-permute-start(bf16[256,256]{1,0:T(8,128)(2,1)S(1)} %collective-permute-done.6), channel_id=1, source_target_pairs={{4,0},{8,4},{12,8},{16,12},{20,16},{24,20},{28,24},{32,28},{36,32}... | collective-permute-start | bytes 393224 | tf_op jit(solution)/shard_map/ppermute | solution.py:15
  50.1 8.8 %collective-permute-start.9 = (bf16[256,1024]{1,0:T(8,128)(2,1)S(1)}, bf16[256,1024]{1,0:T(8,128)(2,1)S(1)}, u32[]{:S(2)}, u32[]{:S(2)}) collective-permute-start(bf16[256,1024]{1,0:T(8,128)(2,1)S(1)} %collective-permute-done.8), channel_id=1, source_target_pairs={{0,4},{4,8},{8,12},{12,16},{16,20},{20,24},{24,28},{28,32},{32,36}... | collective-permute-start | bytes 1572872 | tf_op jit(solution)/shard_map/ppermute | solution.py:15
  53.0 10.8 %collective-permute-start.13 = (bf16[256,1024]{1,0:T(8,128)(2,1)S(1)}, bf16[256,1024]{1,0:T(8,128)(2,1)S(1)}, u32[]{:S(2)}, u32[]{:S(2)}) collective-permute-start(bf16[256,1024]{1,0:T(8,128)(2,1)S(1)} %collective-permute-done.12), channel_id=1, source_target_pairs={{4,0},{8,4},{12,8},{16,12},{20,16},{24,20},{28,24},{32,28},{36,32}... | collective-permute-start | bytes 1572872 | tf_op jit(solution)/shard_map/ppermute | solution.py:15
  59.0 12.4 %collective-permute-start.10 = (bf16[256,1024]{1,0:T(8,128)(2,1)S(1)}, bf16[256,1024]{1,0:T(8,128)(2,1)S(1)}, u32[]{:S(2)}, u32[]{:S(2)}) collective-permute-start(bf16[256,1024]{1,0:T(8,128)(2,1)S(1)} %collective-permute-done.9), channel_id=1, source_target_pairs={{0,4},{4,8},{8,12},{12,16},{16,20},{20,24},{24,28},{28,32},{32,36}... | collective-permute-start | bytes 1572872 | tf_op jit(solution)/shard_map/ppermute | solution.py:15
  63.8 10.8 %collective-permute-start.14 = (bf16[256,1024]{1,0:T(8,128)(2,1)S(1)}, bf16[256,1024]{1,0:T(8,128)(2,1)S(1)}, u32[]{:S(2)}, u32[]{:S(2)}) collective-permute-start(bf16[256,1024]{1,0:T(8,128)(2,1)S(1)} %collective-permute-done.13), channel_id=1, source_target_pairs={{4,0},{8,4},{12,8},{16,12},{20,16},{24,20},{28,24},{32,28},{36,32}... | collective-permute-start | bytes 1572872 | tf_op jit(solution)/shard_map/ppermute | solution.py:15
  71.4 12.6 %collective-permute-start.11 = (bf16[256,1024]{1,0:T(8,128)(2,1)S(1)}, bf16[256,1024]{1,0:T(8,128)(2,1)S(1)}, u32[]{:S(2)}, u32[]{:S(2)}) collective-permute-start(bf16[256,1024]{1,0:T(8,128)(2,1)S(1)} %collective-permute-done.10), channel_id=1, source_target_pairs={{0,4},{4,8},{8,12},{12,16},{16,20},{20,24},{24,28},{28,32},{32,36}... | collective-permute-start | bytes 1572872 | tf_op jit(solution)/shard_map/ppermute | solution.py:15
  73.8 10.3 %copy-start.2 = (bf16[256,1024]{1,0:T(8,128)(2,1)S(1)}, bf16[256,1024]{1,0:T(8,128)(2,1)}, u32[]{:S(2)}) copy-start(bf16[256,1024]{1,0:T(8,128)(2,1)} %param.3) | copy-start | bytes 1572868
  74.6 10.9 %collective-permute-start.15 = (bf16[256,1024]{1,0:T(8,128)(2,1)S(1)}, bf16[256,1024]{1,0:T(8,128)(2,1)S(1)}, u32[]{:S(2)}, u32[]{:S(2)}) collective-permute-start(bf16[256,1024]{1,0:T(8,128)(2,1)S(1)} %collective-permute-done.14), channel_id=1, source_target_pairs={{4,0},{8,4},{12,8},{16,12},{20,16},{24,20},{28,24},{32,28},{36,32}... | collective-permute-start | bytes 1572872 | tf_op jit(solution)/shard_map/ppermute | solution.py:15
  89.5 0.7 copy-start.3
  170.8 2.4 %copy-start = (f32[9,256,256]{1,2,0:T(8,128)S(1)}, f32[9,256,256]{1,2,0:T(8,128)}, u32[]{:S(2)}) copy-start(f32[9,256,256]{1,2,0:T(8,128)} %all-reduce.2.cloned.1.call-done) | copy-start | bytes 7077892
Sparse Core Ops, SparseCore 0:
  89.7 81.1 all-reduce.1
where the time goes:
time: 183 us; the launch traced here: 181 us
  waiting for transfers between devices  83.4 us (46%)
  starting transfers between devices  71.3 us (39%)
  between operations  13.8 us (8%)
  other arithmetic  5.87 us (3%)
  matrix products  4.92 us (3%)
  local copies, waits for them, and re-layouts  2.11 us (1%)
    psum x1, waiting for transfers between devices, body(): residual = lax.psum(shard_terms, 'width')  80.6 us
    ppermute x16, starting transfers between devices, passed_along(): return lax.ppermute(block, axis, route)  71.3 us
  transfers between devices with their start and end apart: 17, of which 4 were waited for; matrix products, arithmetic and copies ran while one was open for 2% of the time, Pallas kernels for 0%

commit v1 on v0

v1 whole, which is shorter than its diff:
```python
import functools

import jax
import jax.numpy as jnp
from jax import lax
from jax.experimental import pallas as pl
from jax.experimental.pallas import tpu as pltpu
from jax.sharding import PartitionSpec as P

DT = 4096
DS = 1024
REACH = 4
MESH = pl.DeviceIdType.MESH
CHUNKS = 4
F32 = jnp.float32
BF16 = jnp.bfloat16


def dot(a, b, ca, cb):
    return lax.dot_general(a, b, (((ca,), (cb,)), ((), ())), preferred_element_type=F32)


def kernel(
    batch, width, rows, ks, kt, n,
    t_ref, s_ref, o_ref,
    bbuf, abuf, cbuf, eself, rself, esend, erecv, eselfrecv, rfull,
    acc_a, acc_b, acc_c, msg_c, msg_a, msg_d, got_c, got_a, got_d, hb,
    in_sem, up_send, down_send, a_recv, c_recv, fwd_send, fwd_recv, b_send, b_recv,
    rs_send, rs_recv, ag_send, ag_recv, m_send, m_recv,
):
    k_all = ks + kt
    part = rows // n
    piece = part // width
    me = lax.axis_index("batch")
    wx = lax.axis_index("width")
    core = lax.rem(me, 2)
    chip = me // 2
    has_prev = chip > 0
    has_next = chip < batch // 2 - 1
    prev = (lax.rem(me + batch - 2, batch), wx)
    nxt = (lax.rem(me + 2, batch), wx)
    other = 1 - core
    mate = (me + 1 - 2 * core, wx)

    def peer(d):
        return lax.rem(wx + d, width)

    barrier = pltpu.get_barrier_semaphore()

    def greet(device):
        pl.semaphore_signal(barrier, inc=1, device_id=device, device_id_type=MESH)

    greet(mate)
    for d in range(1, width):
        greet((me, peer(d)))

    @pl.when(has_prev)
    def _():
        greet(prev)

    @pl.when(has_next)
    def _():
        greet(nxt)

    loads = [
        pltpu.make_async_copy(s_ref, bbuf.at[core, :, pl.ds(0, ks)], in_sem.at[0]),
        pltpu.make_async_copy(t_ref, bbuf.at[core, :, pl.ds(ks, kt)], in_sem.at[1]),
    ]
    for c in loads:
        c.start()

    @pl.when(jnp.logical_not(has_prev))
    def _():
        abuf[...] = jnp.zeros_like(abuf)

    @pl.when(jnp.logical_not(has_next))
    def _():
        cbuf[...] = jnp.zeros_like(cbuf)

    for c in loads:
        c.wait()

    pl.semaphore_wait(barrier, width + has_prev.astype(jnp.int32) + has_next.astype(jnp.int32))

    def remote(src, dst, send, recv, device):
        return pltpu.make_async_remote_copy(
            src_ref=src, dst_ref=dst, send_sem=send, recv_sem=recv, device_id=device, device_id_type=MESH
        )

    def own(q):
        return bbuf.at[core, pl.ds(q * part, part)]

    ups = [remote(own(q), abuf.at[q, core], up_send.at[q], a_recv.at[q], nxt) for q in range(n)]
    downs = [remote(own(q), cbuf.at[q], down_send.at[q], c_recv.at[q], prev) for q in range(n)]
    fwds = [remote(abuf.at[q, core], abuf.at[q, core], fwd_send.at[q], fwd_recv.at[q], mate) for q in range(n)]
    share = remote(bbuf.at[core], bbuf.at[core], b_send, b_recv, mate)
    share.start()
    for q in range(n):
        @pl.when(has_next)
        def _(q=q):
            ups[q].start()

        @pl.when(has_prev)
        def _(q=q):
            downs[q].start()

    lane = lax.broadcasted_iota(jnp.int32, (1, k_all), 1)
    signs = jnp.where(lane < ks, -float(DT // DS), 1.0).astype(F32)
    signs_low = signs.astype(BF16)

    def half_norm(x):
        wide = x.astype(F32)
        return 0.5 * jnp.sum(wide * wide * signs, axis=1, keepdims=True)

    def as_row(col):
        m = col.shape[0]
        pieces = [
            jnp.transpose(jnp.broadcast_to(col[i : i + 128], (128, 128)))[0:1, :] for i in range(0, m, 128)
        ]
        return pieces[0] if len(pieces) == 1 else jnp.concatenate(pieces, axis=1)

    scale = 2.0 / DT
    ones = jnp.ones((1, 128), BF16)

    def aug(s):
        return jnp.concatenate([s, jnp.broadcast_to(ones, (s.shape[0], 128))], axis=1)

    widths = [2 * rows] + [2 * rows + 2 * part * (q + 1) + 2 * part * q for q in range(n)]

    def scatter(stage, src, dst):
        cs = [
            remote(src.at[peer(d)], dst.at[d - 1], rs_send.at[stage, d - 1], rs_recv.at[stage, d - 1], (me, peer(d)))
            for d in range(1, width)
        ]
        for c in cs:
            c.start()
        return cs

    def reduce(cs, src, dst, mask):
        total = src[wx].astype(F32)
        for c in cs:
            c.wait_recv()
        for d in range(width - 1):
            total = total + dst[d].astype(F32)
        if mask is not None:
            total = jnp.where(mask, total, 0.0)
        return total.astype(BF16)

    def gather(stage, out, low):
        out[wx] = low
        cs = [
            remote(out.at[wx], out.at[wx], ag_send.at[stage, d - 1], ag_recv.at[stage, d - 1], (me, peer(d)))
            for d in range(1, width)
        ]
        for c in cs:
            c.start()
        return cs

    share.wait_recv()
    for i in range(2):
        hb[:, i * rows : (i + 1) * rows] = as_row(half_norm(bbuf[i]))
    mine = bbuf[core]
    g = dot(mine * signs_low, bbuf[...].reshape(2 * rows, k_all), 1, 1)
    e = (g - half_norm(mine) - hb[...]) * scale
    eself[...] = e.astype(BF16).reshape(width, rows // width, 2 * rows)
    scatters = [scatter(0, eself, eselfrecv)]
    gathers = [None] * (n + 1)

    acc_a[...] = jnp.zeros_like(acc_a)
    acc_b[...] = jnp.zeros_like(acc_b)
    acc_c[...] = jnp.zeros_like(acc_c)
    gathers[0] = gather(0, rself, reduce(scatters[0], eself, eselfrecv, None))

    def pull(stage):
        for c in gathers[stage]:
            c.wait_recv()
        sb = aug(bbuf[:, :, 0:ks].reshape(2 * rows, ks))
        if stage == 0:
            r = rself[...].reshape(rows, 2 * rows)
            acc_b[core] += dot(r, sb, 1, 0)
            return
        q = stage - 1
        r = rfull[q, :, :, 0 : widths[stage]].reshape(part, widths[stage])
        sc = aug(cbuf[q, :, 0:ks])
        sa = aug(abuf[0 : q + 1, :, :, 0:ks].reshape(2 * part * (q + 1), ks))
        rb = r[:, 0 : 2 * rows]
        ra = r[:, 2 * rows : 2 * rows + 2 * part * (q + 1)]
        acc_c[q] += dot(rb, sb, 1, 0) + dot(ra, sa, 1, 0)
        acc_b[...] += dot(rb, sc, 0, 0).reshape(2, rows, ks + 128)
        acc_a[0 : q + 1] += dot(ra, sc, 0, 0).reshape(q + 1, 2, part, ks + 128)
        sa_q = aug(abuf[q, :, :, 0:ks].reshape(2 * part, ks))
        for p in range(q):
            at = 2 * rows + 2 * part * (q + 1 + p)
            rp = r[:, at : at + 2 * part]
            acc_c[p] += dot(rp, sa_q, 1, 0)
            acc_a[q] += dot(rp, aug(cbuf[p, :, 0:ks]), 0, 0).reshape(2, part, ks + 128)

    half_c = []
    half_a = []
    for q in range(n):
        stage = 1 + q

        @pl.when(has_prev)
        def _(q=q):
            ups[q].wait_recv()
            fwds[q].start()

        @pl.when(has_next)
        def _(q=q):
            downs[q].wait_recv()

        @pl.when(has_prev)
        def _(q=q):
            fwds[q].wait_recv()

        c_low = cbuf[q]
        c_scaled = c_low * signs_low
        a_q = abuf[q].reshape(2 * part, k_all)
        half_c.append(half_norm(c_low))
        half_a.append(as_row(half_norm(a_q)))
        gb = dot(c_scaled, bbuf[...].reshape(2 * rows, k_all), 1, 1)
        ga = dot(c_scaled, abuf[0 : q + 1].reshape(2 * part * (q + 1), k_all), 1, 1)
        cols = [(gb - half_c[q] - hb[...])]
        cols.append(ga - half_c[q] - (half_a[0] if q == 0 else jnp.concatenate(half_a, axis=1)))
        for p in range(q):
            gp = dot(cbuf[p] * signs_low, a_q, 1, 1)
            cols.append(gp - half_c[p] - half_a[q])
        at = 0
        for col in cols:
            wide = col.shape[1]
            esend[q, :, :, at : at + wide] = (col * scale).astype(BF16).reshape(width, piece, wide)
            at += wide
        view = lambda ref, q=q: ref.at[q, :, :, pl.ds(0, widths[1 + q])]
        scatters.append(scatter(stage, view(esend), view(erecv)))
        pull(stage - 1)
        lanes = lax.broadcasted_iota(jnp.int32, (1, widths[stage]), 1)
        in_a = lanes >= 2 * rows
        first = lax.rem(lanes // part, 2) == 0
        skip = jnp.logical_and(in_a, jnp.logical_or(jnp.logical_not(has_prev), jnp.logical_and(first, core == 1)))
        mask = jnp.logical_and(has_next, jnp.logical_not(skip))
        low = reduce(scatters[stage], view(esend), view(erecv), mask)
        gathers[stage] = gather(stage, view(rfull), low)
    pull(n)

    def message(s, acc):
        total = acc[:, ks : ks + 128]
        wide = s.astype(F32)
        return jnp.concatenate([wide[:, i : i + 128] * total for i in range(0, ks, 128)], axis=1) - acc[:, 0:ks]

    msg_c[...] = message(cbuf[:, :, 0:ks].reshape(rows, ks), acc_c[...].reshape(rows, ks + 128))
    send_c = remote(msg_c, got_c, m_send.at[0], m_recv.at[0], nxt)

    @pl.when(has_next)
    def _():
        send_c.start()

    msg_d[0] = message(abuf[:, other, :, 0:ks].reshape(rows, ks), acc_a[:, other].reshape(rows, ks + 128))
    msg_d[1] = message(bbuf[other, :, 0:ks], acc_b[other])
    send_d = remote(msg_d, got_d, m_send.at[1], m_recv.at[1], mate)
    send_d.start()
    mine_a = message(abuf[:, core, :, 0:ks].reshape(rows, ks), acc_a[:, core].reshape(rows, ks + 128))
    send_d.wait_recv()
    msg_a[...] = mine_a + got_d[0]
    send_a = remote(msg_a, got_a, m_send.at[2], m_recv.at[2], prev)

    @pl.when(has_prev)
    def _():
        send_a.start()

    near = (2 * REACH + 1) * rows
    o_ref[...] = message(bbuf[core, :, 0:ks], acc_b[core]) + got_d[1]

    @pl.when(has_prev)
    def _():
        send_c.wait_recv()
        o_ref[...] += got_c[...]

    @pl.when(has_next)
    def _():
        send_a.wait_recv()
        o_ref[...] += got_a[...]

    o_ref[...] = o_ref[...] / near

    share.wait_send()
    send_d.wait_send()
    for cs in scatters + gathers:
        for c in cs:
            c.wait_send()

    @pl.when(has_next)
    def _():
        for c in ups:
            c.wait_send()
        send_c.wait_send()

    @pl.when(has_prev)
    def _():
        for c in downs + fwds:
            c.wait_send()
        send_a.wait_send()


def solution(mesh):
    batch, width = mesh.shape["batch"], mesh.shape["width"]
    n = CHUNKS

    def body(teacher, student):
        rows, kt = teacher.shape
        ks = student.shape[1]
        part = rows // n
        k_all = ks + kt
        wide = 2 * rows + 2 * part * (2 * n - 1)
        dma = pltpu.SemaphoreType.DMA
        return pl.pallas_call(
            functools.partial(kernel, batch, width, rows, ks, kt, n),
            out_shape=jax.ShapeDtypeStruct((rows, ks), F32),
            in_specs=[pl.BlockSpec(memory_space=pl.ANY)] * 2,
            out_specs=pl.BlockSpec(memory_space=pltpu.VMEM),
            scratch_shapes=[
                pltpu.VMEM((2, rows, k_all), BF16),
                pltpu.VMEM((n, 2, part, k_all), BF16),
                pltpu.VMEM((n, part, k_all), BF16),
                pltpu.VMEM((width, rows // width, 2 * rows), BF16),
                pltpu.VMEM((width, rows // width, 2 * rows), BF16),
                pltpu.VMEM((n, width, part // width, wide), BF16),
                pltpu.VMEM((n, width - 1, part // width, wide), BF16),
                pltpu.VMEM((width - 1, rows // width, 2 * rows), BF16),
                pltpu.VMEM((n, width, part // width, wide), BF16),
                pltpu.VMEM((n, 2, part, ks + 128), F32),
                pltpu.VMEM((2, rows, ks + 128), F32),
                pltpu.VMEM((n, part, ks + 128), F32),
                pltpu.VMEM((rows, ks), F32),
                pltpu.VMEM((rows, ks), F32),
                pltpu.VMEM((2, rows, ks), F32),
                pltpu.VMEM((rows, ks), F32),
                pltpu.VMEM((rows, ks), F32),
                pltpu.VMEM((2, rows, ks), F32),
                pltpu.VMEM((1, 2 * rows), F32),
                dma((2,)), dma((n,)), dma((n,)), dma((n,)), dma((n,)), dma((n,)), dma((n,)), dma, dma,
                dma((n + 1, width - 1)), dma((n + 1, width - 1)), dma((n + 1, width - 1)), dma((n + 1, width - 1)),
                dma((3,)), dma((3,)),
            ],
            compiler_params=pltpu.CompilerParams(
                collective_id=0, has_side_effects=True, vmem_limit_bytes=40 * 2**20
            ),
        )(teacher, student)

    specs = (P("batch", "width"), P("batch", "width"))
    return jax.shard_map(body, mesh=mesh, in_specs=specs, out_specs=P("batch", "width"), check_vma=False)
```

time: 183 us -> 62.9 us (0.34)
  waiting for transfers between devices: 83.4 us -> 0 us
  starting transfers between devices: 71.3 us -> 0 us
  Pallas kernels: 0 us -> 59.7 us
  between operations: 13.8 us -> 0.01 us
  other arithmetic: 5.87 us -> 0 us
  matrix products: 4.92 us -> 0 us
    psum x1 -> x0, waiting for transfers between devices: 80.6 us -> none  [body(): residual = lax.psum(shard_terms, 'width')]
    ppermute x16 -> x0, starting transfers between devices: 71.3 us -> none  [passed_along(): return lax.ppermute(block, axis, route)]
    pallas_call x0 -> x1, Pallas kernels: none -> 59.7 us  [body(): pl.pallas_call(functools.partial(kernel, batch, width, rows, ks, kt, n),...]
    reduce_sum x5 -> x0, other arithmetic: 5.84 us -> none  [the longest x1 2.23 us: body(): row_total = jnp.sum(residual, axis=(0, 2))]
    dot_general x3 -> x0, matrix products: 4.92 us -> none  [the longest x1 3.01 us: body(): jnp.einsum('rk,wck->wrc', teacher, band_teacher, preferred_element_type=j...]
    ppermute x16 -> x0, waiting for transfers between devices: 2.77 us -> none  [passed_along(): return lax.ppermute(block, axis, route)]
  transfers between devices with their start and end apart: 17 -> 0, of which waited for: 4 -> 0; matrix products, arithmetic and copies ran while one was open for 2% -> 0% of each run, Pallas kernels for 0% -> 0%
where the time goes in v1:
time: 62.9 us; the launch traced here: 62.4 us
  Pallas kernels  59.7 us (95%)
  local copies, waits for them, and re-layouts  2.65 us (4%)
    pallas_call x1, Pallas kernels, body(): pl.pallas_call(functools.partial(kernel, batch, width, rows, ks, kt, n),...  59.7 us
    unnamed x5, local copies, waits for them, and re-layouts  2.65 us

profile of v1, /device:TPU:25, one launch (start us, length us, event | category | flops | bytes accessed | tf_op | source)
XLA Modules:
  0.0 62.4 jit_solution(3240935820189597444)
XLA Ops:
  0.0 0.0 copy-start
  0.0 1.0 %copy-done = bf16[256,1024]{1,0:T(8,128)(2,1)S(1)} copy-done((bf16[256,1024]{1,0:T(8,128)(2,1)S(1)}, bf16[256,1024]{1,0:T(8,128)(2,1)}, u32[]{:S(2)}) %copy-start) | copy-done | bytes 524312
  1.0 0.0 copy-start.1
  1.0 0.9 %copy-done.1 = bf16[256,256]{1,0:T(8,128)(2,1)S(1)} copy-done((bf16[256,256]{1,0:T(8,128)(2,1)S(1)}, bf16[256,256]{1,0:T(8,128)(2,1)}, u32[]{:S(2)}) %copy-start.1) | copy-done | bytes 131096
  1.9 59.7 %shard_map.28 = f32[256,256]{1,0:T(8,128)S(1)} custom-call(bf16[256,1024]{1,0:T(8,128)(2,1)S(1)} %copy-done, bf16[256,256]{1,0:T(8,128)(2,1)S(1)} %copy-done.1), custom_call_target="tpu_custom_call" | custom-call | tf_op jit(solution)/shard_map/pallas_call | solution.py:315
  61.7 0.7 %copy.4 = f32[256,256]{1,0:T(8,128)} copy(f32[256,256]{1,0:T(8,128)S(1)} %shard_map.28) | data formatting | bytes 524288
Async XLA Ops:
  0.0 1.0 %copy-start = (bf16[256,1024]{1,0:T(8,128)(2,1)S(1)}, bf16[256,1024]{1,0:T(8,128)(2,1)}, u32[]{:S(2)}) copy-start(bf16[256,1024]{1,0:T(8,128)(2,1)} %t_ref.1) | copy-start | bytes 1572868
  1.0 0.9 %copy-start.1 = (bf16[256,256]{1,0:T(8,128)(2,1)S(1)}, bf16[256,256]{1,0:T(8,128)(2,1)}, u32[]{:S(2)}) copy-start(bf16[256,256]{1,0:T(8,128)(2,1)} %s_ref.1) | copy-start | bytes 393220

commit v2 on v1

v2 whole, which is shorter than its diff:
```python
import functools

import jax
import jax.numpy as jnp
from jax import lax
from jax.experimental import pallas as pl
from jax.experimental.pallas import tpu as pltpu
from jax.sharding import PartitionSpec as P

DT = 4096
DS = 1024
REACH = 4
MESH = pl.DeviceIdType.MESH
CHUNKS = 4
F32 = jnp.float32
BF16 = jnp.bfloat16


def dot(a, b, ca, cb):
    return lax.dot_general(a, b, (((ca,), (cb,)), ((), ())), preferred_element_type=F32)


def kernel(
    batch, width, rows, ks, kt, n,
    t_ref, s_ref, o_ref,
    bbuf, abuf, cbuf, eself, rself, esend, erecv, eselfrecv, rfull,
    acc_a, acc_b, acc_c, sum_a, sum_b, sum_c, sum_own,
    msg_c, msg_a, msg_d, msum_c, msum_a, msum_d,
    got_c, got_a, got_a2, got_d, gsum_c, gsum_a, gsum_a2, gsum_d, hb, col_a,
    in_sem, up_send, down_send, a_recv, c_recv, fwd_send, fwd_recv, b_send, b_recv,
    rs_send, rs_recv, ag_send, ag_recv, m_send, m_recv,
):
    k_all = ks + kt
    part = rows // n
    piece = part // width
    me = lax.axis_index("batch")
    wx = lax.axis_index("width")
    core = lax.rem(me, 2)
    chip = me // 2
    has_prev = chip > 0
    has_next = chip < batch // 2 - 1
    prev = (lax.rem(me + batch - 2, batch), wx)
    nxt = (lax.rem(me + 2, batch), wx)
    other = 1 - core
    mate = (me + 1 - 2 * core, wx)
    cross_out = jnp.logical_and(core == 0, has_prev)
    cross_in = jnp.logical_and(core == 1, has_next)
    before = (lax.rem(me + batch - 1, batch), wx)
    after = (lax.rem(me + 1, batch), wx)

    def peer(d):
        return lax.rem(wx + d, width)

    barrier = pltpu.get_barrier_semaphore()

    def greet(device):
        pl.semaphore_signal(barrier, inc=1, device_id=device, device_id_type=MESH)

    @pl.when(has_prev)
    def _():
        greet(prev)

    @pl.when(has_next)
    def _():
        greet(nxt)

    @pl.when(cross_out)
    def _():
        greet(before)

    @pl.when(cross_in)
    def _():
        greet(after)

    for d in range(1, width):
        greet((me, peer(d)))
    greet(mate)

    loads = [
        pltpu.make_async_copy(s_ref, bbuf.at[core, :, pl.ds(0, ks)], in_sem.at[0]),
        pltpu.make_async_copy(t_ref, bbuf.at[core, :, pl.ds(ks, kt)], in_sem.at[1]),
    ]
    for c in loads:
        c.start()

    @pl.when(jnp.logical_not(has_prev))
    def _():
        abuf[...] = jnp.zeros_like(abuf)

    @pl.when(jnp.logical_not(has_next))
    def _():
        cbuf[...] = jnp.zeros_like(cbuf)

    for ref in (acc_a, acc_b, acc_c, sum_a, sum_b, sum_c):
        ref[...] = jnp.zeros_like(ref)

    for c in loads:
        c.wait()

    as_int = lambda x: x.astype(jnp.int32)
    crossing = jnp.logical_or(cross_out, cross_in)
    pl.semaphore_wait(barrier, width + as_int(has_prev) + as_int(has_next) + as_int(crossing))

    def remote(src, dst, send, recv, device):
        return pltpu.make_async_remote_copy(
            src_ref=src, dst_ref=dst, send_sem=send, recv_sem=recv, device_id=device, device_id_type=MESH
        )

    def own(q):
        return bbuf.at[core, pl.ds(q * part, part)]

    ups = [remote(own(q), abuf.at[q, core], up_send.at[q], a_recv.at[q], nxt) for q in range(n)]
    downs = [remote(own(q), cbuf.at[q], down_send.at[q], c_recv.at[q], prev) for q in range(n)]
    fwds = [remote(abuf.at[q, core], abuf.at[q, core], fwd_send.at[q], fwd_recv.at[q], mate) for q in range(n)]
    share = remote(bbuf.at[core], bbuf.at[core], b_send, b_recv, mate)
    share.start()
    for q in range(n):
        @pl.when(has_next)
        def _(q=q):
            ups[q].start()

        @pl.when(has_prev)
        def _(q=q):
            downs[q].start()

    lane = lax.broadcasted_iota(jnp.int32, (1, k_all), 1)
    signs = jnp.where(lane < ks, -float(DT // DS), 1.0).astype(F32)
    signs_low = signs.astype(BF16)

    def half_norm(x):
        wide = x.astype(F32)
        return 0.5 * jnp.sum(wide * wide * signs, axis=1, keepdims=True)

    def as_row(col):
        m = col.shape[0]
        pieces = [
            jnp.transpose(jnp.broadcast_to(col[i : i + 128, 0:1], (128, 128)))[0:1, :] for i in range(0, m, 128)
        ]
        return pieces[0] if len(pieces) == 1 else jnp.concatenate(pieces, axis=1)

    def as_col(row):
        m = row.shape[1]
        pieces = [jnp.transpose(jnp.broadcast_to(row[0:1, i : i + 128], (128, 128))) for i in range(0, m, 128)]
        return pieces[0] if len(pieces) == 1 else jnp.concatenate(pieces, axis=0)

    scale = 2.0 / DT

    widths = [2 * rows] + [2 * rows + 2 * part * (q + 1) + 2 * part * q for q in range(n)]

    def scatter(stage, src, dst):
        cs = [
            remote(src.at[peer(d)], dst.at[d - 1], rs_send.at[stage, d - 1], rs_recv.at[stage, d - 1], (me, peer(d)))
            for d in range(1, width)
        ]
        for c in cs:
            c.start()
        return cs

    def reduce(cs, src, dst, mask):
        total = src[wx].astype(F32)
        for c in cs:
            c.wait_recv()
        for d in range(width - 1):
            total = total + dst[d].astype(F32)
        if mask is not None:
            total = jnp.where(mask, total, 0.0)
        return total.astype(BF16)

    def gather(stage, out, low):
        out[wx] = low
        cs = [
            remote(out.at[wx], out.at[wx], ag_send.at[stage, d - 1], ag_recv.at[stage, d - 1], (me, peer(d)))
            for d in range(1, width)
        ]
        for c in cs:
            c.start()
        return cs

    scatters = [None] * (n + 1)
    gathers = [None] * (n + 1)

    share.wait_recv()
    for i in range(2):
        hb[:, i * rows : (i + 1) * rows] = as_row(half_norm(bbuf[i]))
    mine = bbuf[core]
    g = dot(mine * signs_low, bbuf[...].reshape(2 * rows, k_all), 1, 1)
    e = (g - half_norm(mine) - hb[...]) * scale
    eself[...] = e.astype(BF16).reshape(width, rows // width, 2 * rows)
    scatters[0] = scatter(0, eself, eselfrecv)

    def view(ref, q):
        return ref.at[q, :, :, pl.ds(0, widths[1 + q])]

    def finish(stage):
        if stage == 0:
            gathers[0] = gather(0, rself, reduce(scatters[0], eself, eselfrecv, None))
            return
        q = stage - 1
        lanes = lax.broadcasted_iota(jnp.int32, (1, widths[stage]), 1)
        in_a = lanes >= 2 * rows
        first = lax.rem(lanes // part, 2) == 0
        skip = jnp.logical_and(in_a, jnp.logical_or(jnp.logical_not(has_prev), jnp.logical_and(first, core == 1)))
        mask = jnp.logical_and(has_next, jnp.logical_not(skip))
        low = reduce(scatters[stage], view(esend, q), view(erecv, q), mask)
        gathers[stage] = gather(stage, view(rfull, q), low)

    def row_sum(r):
        return jnp.broadcast_to(jnp.sum(r.astype(F32), axis=1, keepdims=True), (r.shape[0], 128))

    def col_sum(r):
        return jnp.sum(r.astype(F32), axis=0, keepdims=True)

    def pull(stage):
        for c in gathers[stage]:
            c.wait_recv()
        sb = bbuf[:, :, 0:ks].reshape(2 * rows, ks)
        if stage == 0:
            r = rself[...].reshape(rows, 2 * rows)
            acc_b[core] += dot(r, sb, 1, 0)
            sum_own[...] = row_sum(r)
            return
        q = stage - 1
        r = rfull[q, :, :, 0 : widths[stage]].reshape(part, widths[stage])
        sc = cbuf[q, :, 0:ks]
        sa = abuf[0 : q + 1, :, :, 0:ks].reshape(2 * part * (q + 1), ks)
        sa_q = abuf[q, :, :, 0:ks].reshape(2 * part, ks)
        a_end = 2 * rows + 2 * part * (q + 1)
        rb = r[:, 0 : 2 * rows]
        ra = r[:, 2 * rows : a_end]
        rp = [r[:, a_end + 2 * part * p : a_end + 2 * part * (p + 1)] for p in range(q)]
        acc_c[q] += dot(rb, sb, 1, 0) + dot(ra, sa, 1, 0)
        sum_c[q] += row_sum(r[:, 0:a_end])
        for p in range(q):
            acc_c[p] += dot(rp[p], sa_q, 1, 0)
            sum_c[p] += row_sum(rp[p])
        if stage == n:
            send_rows_c()
        acc_a[0 : q + 1] += dot(ra, sc, 0, 0).reshape(q + 1, 2, part, ks)
        sum_a[0:1, 0 : 2 * part * (q + 1)] += col_sum(ra)
        for p in range(q):
            acc_a[q] += dot(rp[p], cbuf[p, :, 0:ks], 0, 0).reshape(2, part, ks)
            sum_a[0:1, 2 * part * q : 2 * part * (q + 1)] += col_sum(rp[p])
        if stage == n:
            send_rows_a()
        acc_b[...] += dot(rb, sc, 0, 0).reshape(2, rows, ks)
        sum_b[0:1] += col_sum(rb)

    def pair(i, src, dst, ssrc, sdst, device):
        return [
            remote(src, dst, m_send.at[2 * i], m_recv.at[2 * i], device),
            remote(ssrc, sdst, m_send.at[2 * i + 1], m_recv.at[2 * i + 1], device),
        ]

    send_c = pair(0, msg_c, got_c, msum_c, gsum_c, nxt)
    send_a = pair(1, msg_a.at[core], got_a, msum_a, gsum_a, prev)
    send_a2 = pair(2, msg_a.at[other], got_a2, msum_a, gsum_a2, before)
    send_d = pair(3, msg_d, got_d, msum_d, gsum_d, mate)

    def send_rows_c():
        msg_c[...] = acc_c[...].reshape(rows, ks).astype(BF16)
        msum_c[...] = jnp.broadcast_to(as_row(sum_c[...].reshape(rows, 128)), (8, rows))

        @pl.when(has_next)
        def _():
            for c in send_c:
                c.start()

    def send_rows_a():
        for i in range(2):
            msg_a[i] = acc_a[:, i].reshape(rows, ks).astype(BF16)
        msum_a[...] = jnp.broadcast_to(sum_a[0:1], (8, 2 * rows))

        @pl.when(has_prev)
        def _():
            for c in send_a:
                c.start()

        @pl.when(cross_out)
        def _():
            for c in send_a2:
                c.start()

    half_c, half_a = [], []
    for q in range(n):
        stage = 1 + q

        @pl.when(has_prev)
        def _(q=q):
            ups[q].wait_recv()
            fwds[q].start()

        @pl.when(has_next)
        def _(q=q):
            downs[q].wait_recv()

        @pl.when(has_prev)
        def _(q=q):
            fwds[q].wait_recv()

        c_low = cbuf[q]
        c_scaled = c_low * signs_low
        a_q = abuf[q].reshape(2 * part, k_all)
        half_c.append(half_norm(c_low))
        half_a.append(as_row(half_norm(a_q)))
        gb = dot(c_scaled, bbuf[...].reshape(2 * rows, k_all), 1, 1)
        ga = dot(c_scaled, abuf[0 : q + 1].reshape(2 * part * (q + 1), k_all), 1, 1)
        cols = [gb - half_c[q] - hb[...]]
        cols.append(ga - half_c[q] - (half_a[0] if q == 0 else jnp.concatenate(half_a, axis=1)))
        for p in range(q):
            gp = dot(cbuf[p] * signs_low, a_q, 1, 1)
            cols.append(gp - half_c[p] - half_a[q])
        at = 0
        for col in cols:
            wide = col.shape[1]
            esend[q, :, :, at : at + wide] = (col * scale).astype(BF16).reshape(width, piece, wide)
            at += wide
        scatters[stage] = scatter(stage, view(esend, q), view(erecv, q))
        finish(stage - 1)
        if q:
            pull(stage - 2)
    finish(n)
    pull(n - 1)
    pull(n)

    msg_d[...] = acc_b[other]
    msum_d[...] = jnp.broadcast_to(sum_b[0:1], (8, 2 * rows))
    for c in send_d:
        c.start()
    mine_b = acc_b[core]
    cols_of = lambda x, i: x[0:1, i * rows : (i + 1) * rows]
    sums = jnp.where(core == 0, cols_of(sum_b, 0), cols_of(sum_b, 1))
    for c in send_d:
        c.wait_recv()
    sums = sums + jnp.where(core == 0, cols_of(gsum_d, 0), cols_of(gsum_d, 1))
    o_ref[...] = mine_b + got_d[...]

    @pl.when(jnp.logical_not(has_prev))
    def _():
        gsum_c[...] = jnp.zeros_like(gsum_c)

    @pl.when(jnp.logical_not(has_next))
    def _():
        gsum_a[...] = jnp.zeros_like(gsum_a)

    @pl.when(jnp.logical_not(cross_in))
    def _():
        gsum_a2[...] = jnp.zeros_like(gsum_a2)

    @pl.when(cross_in)
    def _():
        for c in send_a2:
            c.wait_recv()
        o_ref[...] += got_a2[...].astype(F32)

    @pl.when(has_prev)
    def _():
        for c in send_c:
            c.wait_recv()
        o_ref[...] += got_c[...].astype(F32)

    @pl.when(has_next)
    def _():
        for c in send_a:
            c.wait_recv()
        o_ref[...] += got_a[...].astype(F32)

    sums = sums + gsum_c[0:1]
    col_a[...] = as_col(gsum_a[0:1] + gsum_a2[0:1]).reshape(n, 2, part, 128)
    total = as_col(sums) + col_a[:, core].reshape(rows, 128) + sum_own[...]
    near = (2 * REACH + 1) * rows
    s_own = bbuf[core, :, 0:ks].astype(F32)
    for i in range(0, ks, 128):
        o_ref[:, i : i + 128] = (s_own[:, i : i + 128] * total - o_ref[:, i : i + 128]) * (1.0 / near)

    share.wait_send()
    for c in send_d:
        c.wait_send()
    for cs in scatters + gathers:
        for c in cs:
            c.wait_send()

    @pl.when(has_next)
    def _():
        for c in ups + send_c:
            c.wait_send()

    @pl.when(has_prev)
    def _():
        for c in downs + fwds + send_a:
            c.wait_send()

    @pl.when(cross_out)
    def _():
        for c in send_a2:
            c.wait_send()


def solution(mesh):
    batch, width = mesh.shape["batch"], mesh.shape["width"]
    n = CHUNKS

    def body(teacher, student):
        rows, kt = teacher.shape
        ks = student.shape[1]
        part = rows // n
        k_all = ks + kt
        wide = 2 * rows + 2 * part * (2 * n - 1)
        dma = pltpu.SemaphoreType.DMA
        return pl.pallas_call(
            functools.partial(kernel, batch, width, rows, ks, kt, n),
            out_shape=jax.ShapeDtypeStruct((rows, ks), F32),
            in_specs=[pl.BlockSpec(memory_space=pl.ANY)] * 2,
            out_specs=pl.BlockSpec(memory_space=pltpu.VMEM),
            scratch_shapes=[
                pltpu.VMEM((2, rows, k_all), BF16),
                pltpu.VMEM((n, 2, part, k_all), BF16),
                pltpu.VMEM((n, part, k_all), BF16),
                pltpu.VMEM((width, rows // width, 2 * rows), BF16),
                pltpu.VMEM((width, rows // width, 2 * rows), BF16),
                pltpu.VMEM((n, width, part // width, wide), BF16),
                pltpu.VMEM((n, width - 1, part // width, wide), BF16),
                pltpu.VMEM((width - 1, rows // width, 2 * rows), BF16),
                pltpu.VMEM((n, width, part // width, wide), BF16),
                pltpu.VMEM((n, 2, part, ks), F32),
                pltpu.VMEM((2, rows, ks), F32),
                pltpu.VMEM((n, part, ks), F32),
                pltpu.VMEM((8, 2 * rows), F32),
                pltpu.VMEM((8, 2 * rows), F32),
                pltpu.VMEM((n, part, 128), F32),
                pltpu.VMEM((rows, 128), F32),
                pltpu.VMEM((rows, ks), BF16),
                pltpu.VMEM((2, rows, ks), BF16),
                pltpu.VMEM((rows, ks), F32),
                pltpu.VMEM((8, rows), F32),
                pltpu.VMEM((8, 2 * rows), F32),
                pltpu.VMEM((8, 2 * rows), F32),
                pltpu.VMEM((rows, ks), BF16),
                pltpu.VMEM((rows, ks), BF16),
                pltpu.VMEM((rows, ks), BF16),
                pltpu.VMEM((rows, ks), F32),
                pltpu.VMEM((8, rows), F32),
                pltpu.VMEM((8, 2 * rows), F32),
                pltpu.VMEM((8, 2 * rows), F32),
                pltpu.VMEM((8, 2 * rows), F32),
                pltpu.VMEM((1, 2 * rows), F32),
                pltpu.VMEM((n, 2, part, 128), F32),
                dma((2,)), dma((n,)), dma((n,)), dma((n,)), dma((n,)), dma((n,)), dma((n,)), dma, dma,
                dma((n + 1, width - 1)), dma((n + 1, width - 1)), dma((n + 1, width - 1)), dma((n + 1, width - 1)),
                dma((8,)), dma((8,)),
            ],
            compiler_params=pltpu.CompilerParams(
                collective_id=0, has_side_effects=True, vmem_limit_bytes=60 * 2**20
            ),
        )(teacher, student)

    specs = (P("batch", "width"), P("batch", "width"))
    return jax.shard_map(body, mesh=mesh, in_specs=specs, out_specs=P("batch", "width"), check_vma=False)
```

time: 62.9 us -> 49.7 us (0.79)
  Pallas kernels: 59.7 us -> 47.8 us
  local copies, waits for them, and re-layouts: 2.65 us -> 1.67 us
    pallas_call x1, Pallas kernels: 59.7 us -> 47.8 us  [body(): pl.pallas_call(functools.partial(kernel, batch, width, rows, ks, kt, n),...]
    unnamed x5 -> x1, local copies, waits for them, and re-layouts: 2.65 us -> 1.67 us
where the time goes in v2:
time: 49.7 us; the launch traced here: 49.5 us
  Pallas kernels  47.8 us (96%)
  local copies, waits for them, and re-layouts  1.67 us (3%)
    pallas_call x1, Pallas kernels, body(): pl.pallas_call(functools.partial(kernel, batch, width, rows, ks, kt, n),...  47.8 us
    unnamed x1, local copies, waits for them, and re-layouts  1.67 us

profile of v2, /device:TPU:25, one launch (start us, length us, event | category | flops | bytes accessed | tf_op | source)
XLA Modules:
  0.0 49.5 jit_solution(7949073242801556688)
XLA Ops:
  0.0 47.8 %shard_map.28 = f32[256,256]{1,0:T(8,128)} custom-call(bf16[256,1024]{1,0:T(8,128)(2,1)} %t_ref.1, bf16[256,256]{1,0:T(8,128)(2,1)} %s_ref.1), custom_call_target="tpu_custom_call" | custom-call | tf_op jit(solution)/shard_map/pallas_call | solution.py:409
  47.8 1.7 %copy.4 = f32[256,256]{1,0:T(8,128)} copy(f32[256,256]{1,0:T(8,128)} %shard_map.28) | data formatting | bytes 524288

commit v3 on v2

v3 whole, which is shorter than its diff:
```python
import functools

import jax
import jax.numpy as jnp
from jax import lax
from jax.experimental import pallas as pl
from jax.experimental.pallas import tpu as pltpu
from jax.sharding import PartitionSpec as P

DT = 4096
DS = 1024
REACH = 4
MESH = pl.DeviceIdType.MESH
CHUNKS = 4
F32 = jnp.float32
BF16 = jnp.bfloat16


def dot(a, b, ca, cb):
    return lax.dot_general(a, b, (((ca,), (cb,)), ((), ())), preferred_element_type=F32)


def kernel(
    batch, width, rows, ks, kt, n,
    t_ref, s_ref, o_ref,
    bbuf, abuf, cbuf, eself, rself, esend, erecv, eselfrecv, rfull,
    acc_a, acc_b, acc_c, acc_o, sum_a, sum_b, sum_c, sum_o,
    msg_c, msg_a, msg_d, msg_x, msum_c, msum_a, msum_d, msum_x,
    got_c, got_a, got_d, got_x, gsum_c, gsum_a, gsum_d, gsum_x, msum_e, gsum_e, hb, col_k,
    in_sem, up_send, down_send, a_recv, c_recv, fwd_send, fwd_recv, b_send, b_recv,
    rs_send, rs_recv, ag_send, ag_recv, m_send, m_recv,
):
    k_all = ks + kt
    part = rows // n
    both = 2 * part
    half = both * n
    piece = part // width
    me = lax.axis_index("batch")
    wx = lax.axis_index("width")
    core = lax.rem(me, 2)
    chip = me // 2
    has_prev = chip > 0
    has_next = chip < batch // 2 - 1
    prev = (lax.rem(me + batch - 2, batch), wx)
    nxt = (lax.rem(me + 2, batch), wx)
    other = 1 - core
    mate = (me + 1 - 2 * core, wx)

    def peer(d):
        return lax.rem(wx + d, width)

    barrier = pltpu.get_barrier_semaphore()

    def greet(device):
        pl.semaphore_signal(barrier, inc=1, device_id=device, device_id_type=MESH)

    @pl.when(has_prev)
    def _():
        greet(prev)

    @pl.when(has_next)
    def _():
        greet(nxt)

    for d in range(1, width):
        greet((me, peer(d)))
    greet(mate)

    loads = []
    for q in range(n):
        span = pl.ds(q * part, part)
        loads.append(pltpu.make_async_copy(s_ref.at[span], bbuf.at[q, core, :, pl.ds(0, ks)], in_sem.at[2 * q]))
        loads.append(pltpu.make_async_copy(t_ref.at[span], bbuf.at[q, core, :, pl.ds(ks, kt)], in_sem.at[2 * q + 1]))
    for c in loads:
        c.start()

    @pl.when(jnp.logical_not(has_prev))
    def _():
        abuf[...] = jnp.zeros_like(abuf)
        gsum_c[...] = jnp.zeros_like(gsum_c)

    @pl.when(jnp.logical_not(has_next))
    def _():
        cbuf[...] = jnp.zeros_like(cbuf)
        gsum_a[...] = jnp.zeros_like(gsum_a)

    for ref in (acc_a, acc_b, acc_c, sum_a, sum_b, sum_c):
        ref[...] = jnp.zeros_like(ref)

    for c in loads:
        c.wait()

    as_int = lambda x: x.astype(jnp.int32)
    pl.semaphore_wait(barrier, width + as_int(has_prev) + as_int(has_next))

    def remote(src, dst, send, recv, device):
        return pltpu.make_async_remote_copy(
            src_ref=src, dst_ref=dst, send_sem=send, recv_sem=recv, device_id=device, device_id_type=MESH
        )

    ups = [remote(bbuf.at[q, core], abuf.at[q, core], up_send.at[q], a_recv.at[q], nxt) for q in range(n)]
    downs = [remote(bbuf.at[q, core], cbuf.at[q], down_send.at[q], c_recv.at[q], prev) for q in range(n)]
    fwds = [remote(abuf.at[q, core], abuf.at[q, core], fwd_send.at[q], fwd_recv.at[q], mate) for q in range(n)]
    shares = [remote(bbuf.at[q, core], bbuf.at[q, core], b_send.at[q], b_recv.at[q], mate) for q in range(n)]
    for q in range(n):
        @pl.when(has_next)
        def _(q=q):
            ups[q].start()

        @pl.when(has_prev)
        def _(q=q):
            downs[q].start()

        shares[q].start()

    lane = lax.broadcasted_iota(jnp.int32, (1, k_all), 1)
    signs = jnp.where(lane < ks, -float(DT // DS), 1.0).astype(F32)
    signs_low = signs.astype(BF16)

    def half_norm(x):
        wide = x.astype(F32)
        return 0.5 * jnp.sum(wide * wide * signs, axis=1, keepdims=True)

    def as_row(col):
        m = col.shape[0]
        pieces = [
            jnp.transpose(jnp.broadcast_to(col[i : i + 128, 0:1], (128, 128)))[0:1, :] for i in range(0, m, 128)
        ]
        return pieces[0] if len(pieces) == 1 else jnp.concatenate(pieces, axis=1)

    def as_col(row):
        m = row.shape[1]
        pieces = [jnp.transpose(jnp.broadcast_to(row[0:1, i : i + 128], (128, 128))) for i in range(0, m, 128)]
        return pieces[0] if len(pieces) == 1 else jnp.concatenate(pieces, axis=0)

    def join(parts, axis):
        return parts[0] if len(parts) == 1 else jnp.concatenate(parts, axis=axis)

    scale = 2.0 / DT

    def scatter(i, src, dst):
        cs = [
            remote(src.at[peer(d)], dst.at[d - 1], rs_send.at[i, d - 1], rs_recv.at[i, d - 1], (me, peer(d)))
            for d in range(1, width)
        ]
        for c in cs:
            c.start()
        return cs

    def reduce(cs, src, dst, mask):
        total = src[wx].astype(F32)
        for c in cs:
            c.wait_recv()
        for d in range(width - 1):
            total = total + dst[d].astype(F32)
        if mask is not None:
            total = jnp.where(mask, total, 0.0)
        return total.astype(BF16)

    def gather(stage, out, low):
        out[wx] = low
        cs = [
            remote(out.at[wx], out.at[wx], ag_send.at[stage, d - 1], ag_recv.at[stage, d - 1], (me, peer(d)))
            for d in range(1, width)
        ]
        for c in cs:
            c.start()
        return cs

    scatters = [None] * (n + 1)
    gathers = [None] * (n + 1)

    half_o = []
    for q in range(n):
        shares[q].wait_recv()
        hb[:, q * both : (q + 1) * both] = as_row(half_norm(bbuf[q].reshape(both, k_all)))
        half_o.append(half_norm(bbuf[q, core]))
    mid, span = rows // 2, n // 2

    def half_block(ref, i, k, wide):
        return ref[pl.ds(i * span, span), k, :, 0:wide].reshape(mid, wide)

    match = [lax.rem(i + core, 2) for i in range(2)]

    def half_blocks(wide):
        own_halves = [half_block(bbuf, i, core, wide) for i in range(2)]
        return own_halves, [half_block(bbuf, match[i], other, wide) for i in range(2)]

    mine, theirs = half_blocks(k_all)
    norm_m = [half_norm(x) for x in mine]
    row_m = [as_row(x) for x in norm_m]
    row_t = [as_row(half_norm(x)) for x in theirs]
    pairs = [(0, mine[0], row_m[0]), (1, mine[0], row_m[0]), (1, mine[1], row_m[1])]
    pairs += [(0, theirs[0], row_t[0]), (1, theirs[1], row_t[1])]
    for i, (left, right, row) in enumerate(pairs):
        e = (dot(mine[left] * signs_low, right, 1, 1) - norm_m[left] - row) * scale
        eself[:, :, i * mid : (i + 1) * mid] = e.astype(BF16).reshape(width, mid // width, mid)
    scatters[0] = scatter(0, eself, eselfrecv)

    def view(ref, q, at, wide):
        return ref.at[q, :, :, pl.ds(at, wide)]

    def finish(stage):
        if stage == 0:
            gathers[0] = gather(0, rself, reduce(scatters[0], eself, eselfrecv, None))
            return
        q = stage - 1
        lanes = lax.broadcasted_iota(jnp.int32, (1, 2 * half), 1)
        with_b = lanes < both * (n - q)
        b_with_a = lanes >= half + both * (q + 1)
        far = jnp.logical_and(lax.rem(lanes // part, 2) == 0, core == 1)
        c_with_a = jnp.logical_and(jnp.logical_and(has_prev, has_next), jnp.logical_not(far))
        mask = jnp.where(
            with_b, as_int(has_next), jnp.where(b_with_a, as_int(has_prev), as_int(c_with_a))
        )
        gathers[stage] = gather(stage, rfull.at[q], reduce(scatters[stage], esend.at[q], erecv.at[q], mask > 0))

    def row_sum(r):
        return jnp.broadcast_to(jnp.sum(r.astype(F32), axis=1, keepdims=True), (r.shape[0], 128))

    def col_sum(r):
        return jnp.sum(r.astype(F32), axis=0, keepdims=True)

    def pull(stage):
        for c in gathers[stage]:
            c.wait_recv()
        if stage == 0:
            r = rself[...].reshape(mid, 5 * mid)
            r00, r10, r11, x0, x1 = [r[:, i * mid : (i + 1) * mid] for i in range(5)]
            (s0, s1), (t0, t1) = half_blocks(ks)
            acc_o[0:span] = (dot(r00, s0, 1, 0) + dot(r10, s1, 0, 0) + dot(x0, t0, 1, 0)).reshape(span, part, ks)
            acc_o[span:n] = (dot(r10, s0, 1, 0) + dot(r11, s1, 1, 0) + dot(x1, t1, 1, 0)).reshape(span, part, ks)
            sum_o[0:span] = (row_sum(r00) + row_sum(x0) + as_col(col_sum(r10))).reshape(span, part, 128)
            sum_o[span:n] = (row_sum(r10) + row_sum(r11) + row_sum(x1)).reshape(span, part, 128)
            for i, (x, s_i) in enumerate([(x0, s0), (x1, s1)]):
                at = pl.ds(match[i] * span, span)
                acc_b[at, other] += dot(x, s_i, 0, 0).reshape(span, part, ks)
                msum_e[match[i]] = jnp.broadcast_to(col_sum(x), (8, mid))
            return
        q = stage - 1
        last = stage == n
        b_end = both * (n - q)
        r = rfull[q].reshape(part, 2 * half)
        rb, ra = r[:, 0:b_end], r[:, b_end:half]
        rs = join([r[:, half + both * i : half + both * (i + 1)] for i in range(n)], 0)
        sc = cbuf[q, :, 0:ks]
        sa = abuf[q, :, :, 0:ks].reshape(both, ks)
        left = [sc] + [cbuf[p, :, 0:ks] for p in range(q)] + [bbuf[p, core, :, 0:ks] for p in range(q + 1, n)]
        acc_a[q] += dot(rs, join(left, 0), 0, 0).reshape(2, part, ks)
        sum_a[0:1, both * q : both * (q + 1)] += col_sum(rs)
        if q:
            acc_a[0:q] += dot(ra, sc, 0, 0).reshape(q, 2, part, ks)
            sum_a[0:1, 0 : both * q] += col_sum(ra)
        if last:
            send_rows_a()
        x = dot(rs, sa, 1, 0)
        xs = row_sum(rs)
        y = dot(rb, bbuf[q:n, :, :, 0:ks].reshape(b_end, ks), 1, 0)
        if q:
            y += dot(ra, abuf[0:q, :, :, 0:ks].reshape(both * q, ks), 1, 0)
        acc_c[q] += x[0:part] + y
        sum_c[q] += xs[0:part] + row_sum(r[:, 0:half])
        if q:
            acc_c[0:q] += x[part : part * (q + 1)].reshape(q, part, ks)
            sum_c[0:q] += xs[part : part * (q + 1)].reshape(q, part, 128)
        if last:
            send_rows_c()
        acc_b[q:n] += dot(rb, sc, 0, 0).reshape(n - q, 2, part, ks)
        sum_b[0:1, both * q : half] += col_sum(rb)
        if last:
            send_rows_d()
        else:
            acc_o[q + 1 : n] += x[part * (q + 1) :].reshape(n - 1 - q, part, ks)
            sum_o[q + 1 : n] += xs[part * (q + 1) :].reshape(n - 1 - q, part, 128)

    def pair(i, src, dst, ssrc, sdst, device):
        return [
            remote(src, dst, m_send.at[2 * i], m_recv.at[2 * i], device),
            remote(ssrc, sdst, m_send.at[2 * i + 1], m_recv.at[2 * i + 1], device),
        ]

    send_c = pair(0, msg_c, got_c, msum_c, gsum_c, nxt)
    send_a = pair(1, msg_a, got_a, msum_a, gsum_a, prev)
    send_x = pair(2, msg_x, got_x, msum_x, gsum_x, mate)
    send_d = pair(3, msg_d, got_d, msum_d, gsum_d, mate)
    send_d.append(remote(msum_e, gsum_e, m_send.at[8], m_recv.at[8], mate))

    def begin(cs):
        for c in cs:
            c.start()

    def arrive(cs):
        for c in cs:
            c.wait_recv()

    def send_rows_a():
        @pl.when(has_prev)
        def _():
            msg_x[...] = acc_a[:, other].reshape(rows, ks)
            msum_x[...] = jnp.broadcast_to(sum_a[0:1], (8, half))
            begin(send_x)

    def send_rows_c():
        @pl.when(has_next)
        def _():
            msg_c[...] = acc_c[...].reshape(rows, ks).astype(BF16)
            msum_c[...] = jnp.broadcast_to(as_row(sum_c[...].reshape(rows, 128)), (8, rows))
            begin(send_c)

        @pl.when(has_prev)
        def _():
            arrive(send_x)
            msg_a[...] = (acc_a[:, core].reshape(rows, ks) + got_x[...]).astype(BF16)
            msum_a[...] = jnp.broadcast_to(sum_a[0:1] + gsum_x[0:1], (8, half))
            begin(send_a)

    def send_rows_d():
        msg_d[...] = acc_b[:, other].reshape(rows, ks)
        msum_d[...] = jnp.broadcast_to(sum_b[0:1], (8, half))
        begin(send_d)

    half_c, half_a = [], []
    for q in range(n):
        stage = 1 + q

        @pl.when(has_prev)
        def _(q=q):
            ups[q].wait_recv()
            fwds[q].start()

        @pl.when(has_next)
        def _(q=q):
            downs[q].wait_recv()

        half_c.append(half_norm(cbuf[q]))

        def put(at, tile):
            wide = tile.shape[1]
            esend[q, :, :, at : at + wide] = (tile * scale).astype(BF16).reshape(width, piece, wide)

        c_scaled = cbuf[q] * signs_low
        b_end = both * (n - q)
        put(0, dot(c_scaled, bbuf[q:n].reshape(b_end, k_all), 1, 1) - half_c[q] - hb[:, both * q : half])
        if q:
            g = dot(c_scaled, abuf[0:q].reshape(both * q, k_all), 1, 1)
            put(b_end, g - half_c[q] - join(half_a, 1))
        scatters[stage] = scatter(2 * q + 1, view(esend, q, 0, half), view(erecv, q, 0, half))

        @pl.when(has_prev)
        def _(q=q):
            fwds[q].wait_recv()

        a_q = abuf[q].reshape(both, k_all)
        half_a.append(as_row(half_norm(a_q)))
        left = [cbuf[q]] + [cbuf[p] for p in range(q)] + [bbuf[p, core] for p in range(q + 1, n)]
        norms = [half_c[q]] + half_c[0:q] + half_o[q + 1 : n]
        g = dot(join(left, 0) * signs_low, a_q, 1, 1)
        for i in range(n):
            put(half + both * i, g[part * i : part * (i + 1)] - norms[i] - half_a[q])
        scatters[stage] += scatter(2 * q + 2, view(esend, q, half, half), view(erecv, q, half, half))
        finish(stage - 1)
        if q:
            pull(stage - 2)
    finish(n)
    pull(n - 1)
    pull(n)

    o_ref[...] = acc_b[:, core].reshape(rows, ks) + acc_o[...].reshape(rows, ks)
    arrive(send_d)
    o_ref[...] += got_d[...]

    @pl.when(has_prev)
    def _():
        arrive(send_c)
        o_ref[...] += got_c[...].astype(F32)

    @pl.when(has_next)
    def _():
        arrive(send_a)
        o_ref[...] += got_a[...].astype(F32)

    col_k[...] = as_col(gsum_a[0:1] + gsum_d[0:1] + sum_b[0:1]).reshape(n, 2, part, 128)
    total = as_col(gsum_c[0:1]) + col_k[:, core].reshape(rows, 128) + sum_o[...].reshape(rows, 128)
    total += join([as_col(gsum_e[i, 0:1]) for i in range(2)], 0)
    near = (2 * REACH + 1) * rows
    s_own = bbuf[:, core, :, 0:ks].reshape(rows, ks).astype(F32)
    for i in range(0, ks, 128):
        o_ref[:, i : i + 128] = (s_own[:, i : i + 128] * total - o_ref[:, i : i + 128]) * (1.0 / near)

    for cs in [shares, send_d] + scatters + gathers:
        for c in cs:
            c.wait_send()

    @pl.when(has_next)
    def _():
        for c in ups + send_c:
            c.wait_send()

    @pl.when(has_prev)
    def _():
        for c in downs + fwds + send_a + send_x:
            c.wait_send()


def solution(mesh):
    batch, width = mesh.shape["batch"], mesh.shape["width"]
    n = CHUNKS

    def body(teacher, student):
        rows, kt = teacher.shape
        ks = student.shape[1]
        part = rows // n
        k_all = ks + kt
        half = 2 * rows
        wide = 2 * half
        dma = pltpu.SemaphoreType.DMA
        low = lambda *shape: pltpu.VMEM(shape, BF16)
        full = lambda *shape: pltpu.VMEM(shape, F32)
        return pl.pallas_call(
            functools.partial(kernel, batch, width, rows, ks, kt, n),
            out_shape=jax.ShapeDtypeStruct((rows, ks), F32),
            in_specs=[pl.BlockSpec(memory_space=pl.ANY)] * 2,
            out_specs=pl.BlockSpec(memory_space=pltpu.VMEM),
            scratch_shapes=[
                low(n, 2, part, k_all), low(n, 2, part, k_all), low(n, part, k_all),
                low(width, rows // 2 // width, 5 * rows // 2), low(width, rows // 2 // width, 5 * rows // 2),
                low(n, width, part // width, wide), low(n, width - 1, part // width, wide),
                low(width - 1, rows // 2 // width, 5 * rows // 2), low(n, width, part // width, wide),
                full(n, 2, part, ks), full(n, 2, part, ks), full(n, part, ks), full(n, part, ks),
                full(8, half), full(8, half), full(n, part, 128), full(n, part, 128),
                low(rows, ks), low(rows, ks), full(rows, ks), full(rows, ks),
                full(8, rows), full(8, half), full(8, half), full(8, half),
                low(rows, ks), low(rows, ks), full(rows, ks), full(rows, ks),
                full(8, rows), full(8, half), full(8, half), full(8, half),
                full(2, 8, rows // 2), full(2, 8, rows // 2), full(1, half), full(n, 2, part, 128),
                dma((2 * n,)), dma((n,)), dma((n,)), dma((n,)), dma((n,)), dma((n,)), dma((n,)), dma((n,)), dma((n,)),
                dma((2 * n + 1, width - 1)), dma((2 * n + 1, width - 1)),
                dma((n + 1, width - 1)), dma((n + 1, width - 1)),
                dma((9,)), dma((9,)),
            ],
            compiler_params=pltpu.CompilerParams(
                collective_id=0, has_side_effects=True, vmem_limit_bytes=60 * 2**20
            ),
        )(teacher, student)

    specs = (P("batch", "width"), P("batch", "width"))
    return jax.shard_map(body, mesh=mesh, in_specs=specs, out_specs=P("batch", "width"), check_vma=False)
```

time: 49.7 us -> 48.1 us (0.968)
  Pallas kernels: 47.8 us -> 46.2 us
    pallas_call x1, Pallas kernels: 47.8 us -> 46.2 us  [body(): pl.pallas_call(functools.partial(kernel, batch, width, rows, ks, kt, n),...]
where the time goes in v3:
time: 48.1 us; the launch traced here: 47.9 us
  Pallas kernels  46.2 us (96%)
  local copies, waits for them, and re-layouts  1.67 us (3%)
    pallas_call x1, Pallas kernels, body(): pl.pallas_call(functools.partial(kernel, batch, width, rows, ks, kt, n),...  46.2 us
    unnamed x1, local copies, waits for them, and re-layouts  1.67 us

profile of v3, /device:TPU:25, one launch (start us, length us, event | category | flops | bytes accessed | tf_op | source)
XLA Modules:
  0.0 47.9 jit_solution(12388432125194967132)
XLA Ops:
  0.0 46.2 %shard_map.28 = f32[256,256]{1,0:T(8,128)} custom-call(bf16[256,1024]{1,0:T(8,128)(2,1)} %t_ref.1, bf16[256,256]{1,0:T(8,128)(2,1)} %s_ref.1), custom_call_target="tpu_custom_call" | custom-call | tf_op jit(solution)/shard_map/pallas_call | solution.py:419
  46.2 1.7 %copy.4 = f32[256,256]{1,0:T(8,128)} copy(f32[256,256]{1,0:T(8,128)} %shard_map.28) | data formatting | bytes 524288

commit v4 on v3

--- a/solution.py
+++ b/solution.py
@@ -102,6 +102,8 @@
     downs = [remote(bbuf.at[q, core], cbuf.at[q], down_send.at[q], c_recv.at[q], prev) for q in range(n)]
     fwds = [remote(abuf.at[q, core], abuf.at[q, core], fwd_send.at[q], fwd_recv.at[q], mate) for q in range(n)]
     shares = [remote(bbuf.at[q, core], bbuf.at[q, core], b_send.at[q], b_recv.at[q], mate) for q in range(n)]
+    for c in shares:
+        c.start()
     for q in range(n):
         @pl.when(has_next)
         def _(q=q):
@@ -110,8 +112,6 @@
         @pl.when(has_prev)
         def _(q=q):
             downs[q].start()
-
-        shares[q].start()
 
     lane = lax.broadcasted_iota(jnp.int32, (1, k_all), 1)
     signs = jnp.where(lane < ks, -float(DT // DS), 1.0).astype(F32)
@@ -138,13 +138,15 @@
 
     scale = 2.0 / DT
 
+    far_first = sorted(range(width - 1), key=lambda i: -min(i + 1, width - 1 - i))
+
     def scatter(i, src, dst):
         cs = [
             remote(src.at[peer(d)], dst.at[d - 1], rs_send.at[i, d - 1], rs_recv.at[i, d - 1], (me, peer(d)))
             for d in range(1, width)
         ]
-        for c in cs:
-            c.start()
+        for i in far_first:
+            cs[i].start()
         return cs
 
     def reduce(cs, src, dst, mask):
@@ -163,8 +165,8 @@
             remote(out.at[wx], out.at[wx], ag_send.at[stage, d - 1], ag_recv.at[stage, d - 1], (me, peer(d)))
             for d in range(1, width)
         ]
-        for c in cs:
-            c.start()
+        for i in far_first:
+            cs[i].start()
         return cs
 
     scatters = [None] * (n + 1)
@@ -213,7 +215,12 @@
         mask = jnp.where(
             with_b, as_int(has_next), jnp.where(b_with_a, as_int(has_prev), as_int(c_with_a))
         )
-        gathers[stage] = gather(stage, rfull.at[q], reduce(scatters[stage], esend.at[q], erecv.at[q], mask > 0))
+        gathers[stage] = []
+        for h in range(2):
+            cs = scatters[stage][h * (width - 1) : (h + 1) * (width - 1)]
+            send, recv, out = [view(ref, q, h * half, half) for ref in (esend, erecv, rfull)]
+            low = reduce(cs, send, recv, mask[:, h * half : (h + 1) * half] > 0)
+            gathers[stage] += gather(1 + 2 * q + h, out, low)
 
     def row_sum(r):
         return jnp.broadcast_to(jnp.sum(r.astype(F32), axis=1, keepdims=True), (r.shape[0], 128))
@@ -359,8 +366,9 @@
             put(half + both * i, g[part * i : part * (i + 1)] - norms[i] - half_a[q])
         scatters[stage] += scatter(2 * q + 2, view(esend, q, half, half), view(erecv, q, half, half))
         finish(stage - 1)
-        if q:
-            pull(stage - 2)
+        if q > 1:
+            pull(stage - 3)
+    pull(n - 2)
     finish(n)
     pull(n - 1)
     pull(n)
@@ -435,7 +443,7 @@
                 full(2, 8, rows // 2), full(2, 8, rows // 2), full(1, half), full(n, 2, part, 128),
                 dma((2 * n,)), dma((n,)), dma((n,)), dma((n,)), dma((n,)), dma((n,)), dma((n,)), dma((n,)), dma((n,)),
                 dma((2 * n + 1, width - 1)), dma((2 * n + 1, width - 1)),
-                dma((n + 1, width - 1)), dma((n + 1, width - 1)),
+                dma((2 * n + 1, width - 1)), dma((2 * n + 1, width - 1)),
                 dma((9,)), dma((9,)),
             ],
             compiler_params=pltpu.CompilerParams(

time: 48.1 us -> 46.8 us (0.973)
  Pallas kernels: 46.2 us -> 44.8 us
    pallas_call x1, Pallas kernels: 46.2 us -> 44.8 us  [body(): pl.pallas_call(functools.partial(kernel, batch, width, rows, ks, kt, n),...]
where the time goes in v4:
time: 46.8 us; the launch traced here: 46.5 us
  Pallas kernels  44.8 us (96%)
  local copies, waits for them, and re-layouts  1.67 us (4%)
    pallas_call x1, Pallas kernels, body(): pl.pallas_call(functools.partial(kernel, batch, width, rows, ks, kt, n),...  44.8 us
    unnamed x1, local copies, waits for them, and re-layouts  1.67 us

profile of v4, /device:TPU:25, one launch (start us, length us, event | category | flops | bytes accessed | tf_op | source)
XLA Modules:
  0.0 46.5 jit_solution(12550148688830854528)
XLA Ops:
  0.0 44.8 %shard_map.28 = f32[256,256]{1,0:T(8,128)} custom-call(bf16[256,1024]{1,0:T(8,128)(2,1)} %t_ref.1, bf16[256,256]{1,0:T(8,128)(2,1)} %s_ref.1), custom_call_target="tpu_custom_call" | custom-call | tf_op jit(solution)/shard_map/pallas_call | solution.py:427
  44.8 1.7 %copy.4 = f32[256,256]{1,0:T(8,128)} copy(f32[256,256]{1,0:T(8,128)} %shard_map.28) | data formatting | bytes 524288

commit v5 on v4

--- a/solution.py
+++ b/solution.py
@@ -311,15 +311,17 @@
         @pl.when(has_next)
         def _():
             msg_c[...] = acc_c[...].reshape(rows, ks).astype(BF16)
+            begin(send_c[:1])
             msum_c[...] = jnp.broadcast_to(as_row(sum_c[...].reshape(rows, 128)), (8, rows))
-            begin(send_c)
+            begin(send_c[1:])
 
         @pl.when(has_prev)
         def _():
             arrive(send_x)
             msg_a[...] = (acc_a[:, core].reshape(rows, ks) + got_x[...]).astype(BF16)
+            begin(send_a[:1])
             msum_a[...] = jnp.broadcast_to(sum_a[0:1] + gsum_x[0:1], (8, half))
-            begin(send_a)
+            begin(send_a[1:])
 
     def send_rows_d():
         msg_d[...] = acc_b[:, other].reshape(rows, ks)

time: 46.8 us -> 46.7 us (level)
  no operation moved by 1% of the time
where the time goes in v5:
time: 46.7 us; the launch traced here: 46.5 us
  Pallas kernels  44.8 us (96%)
  local copies, waits for them, and re-layouts  1.67 us (4%)
    pallas_call x1, Pallas kernels, body(): pl.pallas_call(functools.partial(kernel, batch, width, rows, ks, kt, n),...  44.8 us
    unnamed x1, local copies, waits for them, and re-layouts  1.67 us

profile of v5, /device:TPU:25, one launch (start us, length us, event | category | flops | bytes accessed | tf_op | source)
XLA Modules:
  0.0 46.5 jit_solution(17393059571374305528)
XLA Ops:
  0.0 44.8 %shard_map.28 = f32[256,256]{1,0:T(8,128)} custom-call(bf16[256,1024]{1,0:T(8,128)(2,1)} %t_ref.1, bf16[256,256]{1,0:T(8,128)(2,1)} %s_ref.1), custom_call_target="tpu_custom_call" | custom-call | tf_op jit(solution)/shard_map/pallas_call | solution.py:429
  44.8 1.7 %copy.4 = f32[256,256]{1,0:T(8,128)} copy(f32[256,256]{1,0:T(8,128)} %shard_map.28) | data formatting | bytes 524288
